TPU v7x, 32 devices: a whole 2x2x4 slice. The times are simulated.
32 devices in a mesh: row: 4 (over y, x), col: 8 (over z, core).
Axes of the slice: x: 2, y: 2, z: 4, core: 2. Of those that a mesh axis runs over, the one named last changes fastest.
Arguments:
- voltages: bfloat16 [2, 64, 64, 2, 31744], P(None, 'row', 'col'), may hold values from -6 to 6
- fir: float32 [16, 1024], replicated, may hold values from -0.046875 to 0.046875
Outputs:
- power: float32 [64, 64, 2, 1024], P('col', None, None, 'row')
All inputs are finite; a program needn't handle non-finite values.
Results may differ from a plain program's by a relative error of at most 0.0032.
Values may be sent and summed in bfloat16 or wider, within the bound.
A program may use at most 448 MiB of HBM per device.

v0:
```python
import math

import jax
import jax.numpy as jnp
from jax import lax
from jax.sharding import PartitionSpec as P

NROW = 64
NCOL = 64
FRAMES = 16


def float_table(length):
    index = jnp.arange(length, dtype=jnp.int32)
    angle = (index[:, None] * index[None, :] % length).astype(jnp.float32) * (
        2.0 * math.pi / length
    )
    cosine = jnp.cos(angle)
    sine = jnp.sin(angle)
    return jnp.stack([jnp.stack([cosine, -sine]), jnp.stack([sine, cosine])])


def spatial_table(length):
    index = jnp.arange(length, dtype=jnp.int32)
    angle = (index[:, None] * index[None, :] % length).astype(jnp.float32) * (
        2.0 * math.pi / length
    )
    cosine = jnp.cos(angle).astype(jnp.bfloat16)
    sine = jnp.sin(angle).astype(jnp.bfloat16)
    return jnp.stack([jnp.stack([cosine, -sine]), jnp.stack([sine, cosine])])


def row_transform(piece):
    table = spatial_table(piece.shape[1])
    return jnp.einsum(
        "cxbpfhl,cdux->dubpfhl", piece, table, preferred_element_type=jnp.float32
    ).astype(jnp.bfloat16)


def col_transform(piece):
    table = spatial_table(piece.shape[2])
    return jnp.einsum("cubpfhl,cdvb->duvpfhl", piece, table, preferred_element_type=jnp.float32)


def body(voltages, fir):
    taps, nchan = fir.shape
    comps, local_rows, local_cols, pols, samples = voltages.shape
    blocks = samples // nchan
    frames = blocks - taps + 1
    outer_count = lax.axis_size("row")
    inner_count = nchan // outer_count
    shaped = voltages.reshape(comps, local_rows, local_cols, pols, blocks, nchan)
    filtered = jnp.zeros((comps, local_rows, local_cols, pols, frames, nchan), jnp.float32)
    for tap in range(taps):
        filtered = (
            filtered + shaped[:, :, :, :, tap : tap + frames, :].astype(jnp.float32) * fir[tap]
        )
    flat_rows = local_rows * local_cols * pols * frames
    filtered = filtered.reshape(comps, flat_rows, nchan)
    channels = jnp.einsum(
        "cxn,cdnk->dxk",
        filtered,
        float_table(nchan),
        precision=lax.Precision.HIGHEST,
        preferred_element_type=jnp.float32,
    )
    scale = 1.0 / (FRAMES * NROW * NCOL)
    spectra = channels.astype(jnp.bfloat16).reshape(
        comps, local_rows, local_cols, pols, frames, outer_count, inner_count
    )
    rowbeam = row_transform(lax.all_to_all(spectra, "row", split_axis=5, concat_axis=1, tiled=True))
    beams = col_transform(lax.all_to_all(rowbeam, "col", split_axis=1, concat_axis=2, tiled=True))
    summed = jnp.sum(beams * beams, axis=(0, 4)) * scale
    return summed.reshape(
        summed.shape[0], summed.shape[1], summed.shape[2], summed.shape[3] * summed.shape[4]
    )


def solution(mesh):
    in_specs = (P(None, "row", "col", None, None), P())
    out_specs = P("col", None, None, "row")
    return jax.shard_map(body, mesh=mesh, in_specs=in_specs, out_specs=out_specs, check_vma=False)
```

profile of v0, /device:TPU:11, one launch (start us, length us, event | category | flops | bytes accessed | tf_op | source)
XLA Modules:
  0.0 1351.0 jit_solution(98678069368810733)
XLA Ops:
  0.0 17.5 %fusion.17 = (f32[1,1024,1024]{1,2,0:T(8,128)}, f32[1,1024,1024]{1,2,0:T(8,128)}) fusion(), kind=kLoop, calls=%fused_computation.24 | loop fusion | flops 14680064 | bytes 8388608 | tf_op jit(solution)/shard_map/sin | solution.py:19
  17.5 16.5 %fusion.19 = f32[1,1024,1024]{1,2,0:T(8,128)} fusion(), kind=kLoop, calls=%fused_computation.26 | loop fusion | flops 15728640 | bytes 4194304 | tf_op jit(solution)/shard_map/neg | solution.py:20
  34.0 66.1 %reshape.217 = bf16[2,16,8,2,31,1024]{5,4,3,2,1,0:T(8,128)(2,1)} reshape(bf16[2,16,8,2,31744]{4,3,2,1,0:T(2,128)(2,1)} %param.2) | data formatting | bytes 65011712 | tf_op jit(solution)/shard_map/reshape | solution.py:52
  100.0 209.4 %fusion.30 = (bf16[2,16,8,2,16,1024]{5,4,3,2,1,0:T(8,128)(2,1)}, bf16[2,16,8,2,16,1024]{5,4,3,2,1,0:T(8,128)(2,1)}, bf16[2,16,8,2,16,1024]{5,4,3,2,1,0:T(8,128)(...) fusion(bf16[2,16,8,2,31,1024]{5,4,3,2,1,0:T(8,128)(2,1)} %resha, ...), kind=kLoop, calls=%fused_computation.46 | loop fusion | bytes 536870912 | tf_op jit(solution)/shard_map/slice | solution.py:56
  309.5 99.3 %multiply_add_fusion = f32[2,16,8,2,16,1024]{5,4,2,3,1,0:T(8,128)} fusion(bf16[2,16,8,2,16,1024]{5,4,3,2,1,0:T(8,128)(2,1)} %get-tuple-element.20, bf16[2,16,8,2,16,1024]{5,4,3,2,1,0:T(8,128)(2,1)} %get-tuple-element.6, bf16[2,16,8,2,16,1024]{5,4,3,2,1,0:T(8,128)(2,1)} %get-tuple-element.7, bf16[2,16,8,2,16,1024]{5,4,3,2,1,0:T(8,128)(2,1)} %get-tuple-element.8, ...), kind=kLoop, calls=%fused_computation.4 | loop fusion | flops 394264576 | bytes 302055424 | tf_op jit(solution)/shard_map/add | solution.py:56
  408.9 0.0 copy-start
  408.9 0.0 copy-start.1
  408.9 25.7 %copy.23 = f32[2,16,8,2,16,1024]{5,4,3,2,1,0:T(8,128)} copy(f32[2,16,8,2,16,1024]{5,4,2,3,1,0:T(8,128)} %multiply_add_fusion) | data formatting | bytes 67108864 | tf_op jit(solution)/shard_map/add | solution.py:56
  434.6 6.7 maximum_bitcast_fusion
  441.3 232.5 %fusion.1 = bf16[2,4096,1024]{1,2,0:T(8,128)(2,1)} fusion(f32[2,4096,1024,1]{2,1,0,3:T(8,128)} %bitcast.78, f32[1,2,1024,1024]{2,3,0,1:T(8,128)} %get-tuple-element.22, f32[1,2,1024,1024]{2,3,0,1:T(8,128)} %get-tuple-element.21), kind=kOutput, calls=%fused_computation.5 | convolution fusion | flops 206171013120 | bytes 67108864 | tf_op jit(solution)/shard_map/cxn,cdnk->dxk/dot_general | solution.py:60
  673.8 21.2 %copy.24 = bf16[2,4096,1024]{2,1,0:T(8,128)(2,1)} copy(bf16[2,4096,1024]{1,2,0:T(8,128)(2,1)} %fusion.1) | data formatting | bytes 33554432 | tf_op jit(solution)/shard_map/convert_element_type | solution.py:68
  695.0 27.9 %reshape.207 = bf16[2,16,8,2,16,4,256]{6,5,4,3,2,1,0:T(4,128)(2,1)} reshape(bf16[2,4096,1024]{2,1,0:T(8,128)(2,1)} %copy.24) | data formatting | bytes 33554432 | tf_op jit(solution)/shard_map/reshape | solution.py:68
  722.9 15.3 %copy.25 = bf16[2,16,8,2,16,4,256]{6,4,3,2,1,0,5:T(8,128)(2,1)} copy(bf16[2,16,8,2,16,4,256]{6,5,4,3,2,1,0:T(4,128)(2,1)} %reshape.207) | data formatting | bytes 33554432 | tf_op jit(solution)/shard_map/reshape | solution.py:68
  738.2 7.3 all-to-all-start
  745.5 0.1 fusion.26
  745.6 0.2 sine_convert_fusion
  745.8 181.1 %all-to-all-done = bf16[2,16,8,2,16,4,256]{6,4,3,2,1,0,5:T(8,128)(2,1)} async-done(((bf16[2,16,8,2,16,4,256]{6,4,3,2,1,0,5:T(8,128)(2,1)}), bf16[2,16,8,2,16,4,256]{6,4,3,2,1,0,5:T(8,128)(2,1)}, u32[]{:S(2)}, u32[]{:S(2)}) %all-to-all-start) | async-done | bytes 16777248 | tf_op jit(solution)/shard_map/all_to_all | solution.py:71
  926.9 17.9 %copy.26 = bf16[2,4,16,8,2,16,1,256]{7,2,1,0,5,4,3,6:T(8,128)(2,1)} copy(bf16[2,4,16,8,2,16,1,256]{7,5,4,3,2,0,1,6:T(8,128)(2,1)} %bitcast.31) | data formatting | bytes 33554432 | tf_op jit(solution)/shard_map/all_to_all | solution.py:71
  944.8 11.6 fusion.8
  956.3 10.3 copy.27
  966.6 367.7 %all_to_all.30 = bf16[2,64,8,2,16,1,256]{6,4,3,2,0,5,1:T(8,128)(2,1)} all-to-all(bf16[2,64,8,2,16,1,256]{6,4,3,2,0,5,1:T(8,128)(2,1)S(1)} %copy.27), channel_id=1, replica_groups=mesh['row'=4,'col'=8] {'col'}, dimensions={1} | all-to-all | bytes 33554432 | tf_op jit(solution)/shard_map/all_to_all | solution.py:72
  1334.3 14.8 %fusion = f32[64,8,2,256]{3,0,2,1:T(8,128)S(1)} fusion(bf16[2,8,8,8,2,16,1,256]{7,5,4,3,0,2,1,6:T(8,128)(2,1)} %bitcast.79, bf16[1,2,64,64]{3,2,0,1:T(8,128)(2,1)S(1)} %get-tuple-element.40, bf16[1,2,64,64]{3,2,0,1:T(8,128)(2,1)S(1)} %get-tuple-element.39), kind=kOutput, calls=%fused_computation.1 | convolution fusion | flops 2164064256 | bytes 17858560 | tf_op jit(solution)/shard_map/cubpfhl,cdvb->duvpfhl/dot_general | solution.py:42
  1349.1 0.1 multiply_bitcast_fusion
  1349.2 1.8 copy.29
  (8 shorter events, 0.1 us)
Async XLA Ops:
  100.0 209.4 %copy-start.3 = (f32[16,1024]{1,0:T(8,128)S(1)}, f32[16,1024]{1,0:T(8,128)}, u32[]{:S(2)}) copy-start(f32[16,1024]{1,0:T(8,128)} %param.3) | copy-start | bytes 196612
  408.9 25.8 %copy-start = (f32[1,1024,1024]{1,2,0:T(8,128)S(1)}, f32[1,1024,1024]{1,2,0:T(8,128)}, u32[]{:S(2)}) copy-start(f32[1,1024,1024]{1,2,0:T(8,128)} %get-tuple-element.41) | copy-start | bytes 12582916
  408.9 25.7 %copy-start.1 = (f32[1,1024,1024]{1,2,0:T(8,128)S(1)}, f32[1,1024,1024]{1,2,0:T(8,128)}, u32[]{:S(2)}) copy-start(f32[1,1024,1024]{1,2,0:T(8,128)} %get-tuple-element.42) | copy-start | bytes 12582916
  408.9 25.7 %copy-start.2 = (f32[1,1024,1024]{1,2,0:T(8,128)S(1)}, f32[1,1024,1024]{1,2,0:T(8,128)}, u32[]{:S(2)}) copy-start(f32[1,1024,1024]{1,2,0:T(8,128)} %fusion.19) | copy-start | bytes 12582916
  738.2 188.7 %all-to-all-start = ((bf16[2,16,8,2,16,4,256]{6,4,3,2,1,0,5:T(8,128)(2,1)}), bf16[2,16,8,2,16,4,256]{6,4,3,2,1,0,5:T(8,128)(2,1)}, u32[]{:S(2)}, u32[]{:S(2)}) async-start(bf16[2,16,8,2,16,4,256]{6,4,3,2,1,0,5:T(8,128)(2,1)} %copy.25), calls=%async_computation | async-start | bytes 33554432 | tf_op jit(solution)/shard_map/all_to_all | solution.py:71
where the time goes:
time: 1360 us; the launch traced here: 1350 us
  local copies, waits for them, and re-layouts  396 us (29%)
  blocking collectives  368 us (27%)
  matrix products  259 us (19%)
  waiting for transfers between devices  181 us (13%)
  other arithmetic  140 us (10%)
    all_to_all x1, blocking collectives, body(): lax.all_to_all(rowbeam, 'col', split_axis=1, concat_axis=2, tiled=True)  368 us
    dot_general x1, matrix products, body(): jnp.einsum('cxn,cdnk->dxk', filtered, float_table(nchan), precision=lax.P...  232 us
    slice x1, local copies, waits for them, and re-layouts, body(): shaped[:, :, :, :, tap:tap + frames, :].astype(jnp.float32) * fir[tap]  209 us
    all_to_all x1, waiting for transfers between devices, body(): lax.all_to_all(spectra, 'row', split_axis=5, concat_axis=1, tiled=True)  181 us
    add x1, other arithmetic, body(): filtered + shaped[:, :, :, :, tap:tap + frames, :].astype(jnp.float32) *...  99.3 us
    reshape x1, local copies, waits for them, and re-layouts, body(): voltages.reshape(comps, local_rows, local_cols, pols, blocks, nchan)  66.1 us
    reshape x2, local copies, waits for them, and re-layouts, body(): channels.astype(jnp.bfloat16)  43.2 us
  transfers between devices with their start and end apart: 1, of which 1 were waited for; matrix products, arithmetic and copies ran while one was open for 0% of the time, Pallas kernels for 0%

commit v1 on v0

v1 whole, which is shorter than its diff:
```python
import functools
import math

import jax
import jax.numpy as jnp
import numpy as np
import ml_dtypes
from jax import lax
from jax.experimental import pallas as pl
from jax.experimental.pallas import tpu as pltpu
from jax.sharding import PartitionSpec as P

BF16 = jnp.bfloat16
F32 = jnp.float32
MESH = pl.DeviceIdType.MESH
VMEM_BYTES = 58 * 1024 * 1024
SLOTS = 3
CHUNKS = 8


def fourier_parts(length):
    index = np.arange(length)
    angle = (index[:, None] * index[None, :] % length).astype(np.float32) * np.float32(
        2.0 * math.pi / length
    )
    return np.cos(angle), np.sin(angle)


def channel_table(nchan, row_size):
    cosine, sine = fourier_parts(nchan)
    table = np.stack([np.stack([cosine, -sine]), np.stack([sine, cosine])])
    table = table.reshape(2, 2, nchan, row_size, nchan // row_size).transpose(0, 2, 3, 1, 4)
    return table.reshape(2 * nchan, 2 * nchan).astype(ml_dtypes.bfloat16)


def spatial_parts(length):
    cosine, sine = fourier_parts(length)
    table = np.stack([np.stack([cosine, -sine]), np.stack([sine, cosine])])
    return table.astype(ml_dtypes.bfloat16)


def row_table(nrow, row_size, col_size):
    table = spatial_parts(nrow).reshape(2, 2, col_size, nrow // col_size, row_size, nrow // row_size)
    return table.transpose(2, 1, 3, 4, 0, 5).reshape(2 * nrow, 2 * nrow)


def col_table(ncol, col_size, local_beams):
    table = spatial_parts(ncol).astype(np.float32)
    eye = np.eye(local_beams, dtype=np.float32)
    full = np.einsum("cdvb,uw->duvbcw", table, eye)
    return full.reshape(2 * local_beams * ncol, ncol * 2 * local_beams).astype(ml_dtypes.bfloat16)


def channelize_kernel(volts, fir, table, out, held):
    _, _, _, blocks, rows, nchan = volts.shape
    taps = fir.shape[0]
    frames = blocks - taps + 1
    lanes = 128
    steps = nchan // lanes

    def filter_step(step, carry):
        comp = step // steps
        start = pl.multiple_of((step % steps) * lanes, lanes)
        weights = [
            jnp.broadcast_to(fir[pl.ds(tap, 1), pl.ds(start, lanes)], (rows, lanes))
            for tap in range(taps)
        ]
        values = [
            volts[0, 0, comp, block, :, pl.ds(start, lanes)].astype(F32) for block in range(blocks)
        ]
        dest = pl.multiple_of(step * lanes, lanes)
        for frame in range(frames):
            total = values[frame] * weights[0]
            for tap in range(1, taps):
                total = total + values[frame + tap] * weights[tap]
            held[frame, :, pl.ds(dest, lanes)] = total.astype(BF16)
        return carry

    lax.fori_loop(0, 2 * steps, filter_step, 0)
    width = out.shape[-1]
    filtered = held[...].reshape(frames * rows, 2 * nchan)

    for dest in range(out.shape[0]):
        for comp in range(2):
            start = (2 * dest + comp) * width
            part = jnp.dot(
                filtered, table[:, start : start + width], preferred_element_type=F32
            ).astype(BF16)
            out[dest, 0, :, 0, comp * rows : (comp + 1) * rows, :] = part.reshape(frames, rows, width)


def channelize(volts, fir, table, row_size):
    pols, local_cols, _, blocks, local_rows, nchan = volts.shape
    taps = fir.shape[0]
    frames = blocks - taps + 1
    width = nchan // row_size
    return pl.pallas_call(
        channelize_kernel,
        grid=(pols, local_cols),
        in_specs=[
            pl.BlockSpec((1, 1, 2, blocks, local_rows, nchan), lambda p, b: (p, b, 0, 0, 0, 0)),
            pl.BlockSpec((taps, nchan), lambda p, b: (0, 0)),
            pl.BlockSpec((2 * nchan, 2 * nchan), lambda p, b: (0, 0)),
        ],
        out_specs=pl.BlockSpec(
            (row_size, 1, frames, 1, 2 * local_rows, width), lambda p, b: (0, p, 0, b, 0, 0)
        ),
        out_shape=jax.ShapeDtypeStruct(
            (row_size, pols, frames, local_cols, 2 * local_rows, width), BF16
        ),
        scratch_shapes=[pltpu.VMEM((frames, local_rows, 2 * nchan), BF16)],
        compiler_params=pltpu.CompilerParams(vmem_limit_bytes=VMEM_BYTES),
        name="channelize",
    )(volts, fir, table)


def beam_kernel(
    row_size, col_size, chunks, spectra, row_tab, col_tab, power,
    row_recv, col_send, col_recv,
    row_send_sem, row_recv_sem, row_own_sem, col_send_sem, col_recv_sem, col_own_sem,
):
    my_row = lax.axis_index("row")
    my_col = lax.axis_index("col")
    units = spectra.shape[1]
    local_cols = spectra.shape[2]
    width = spectra.shape[4]
    size = units // chunks
    per_pol = units // power.shape[0]
    out_rows = power.shape[1]
    row_peers = [lax.rem(my_row + step, row_size) for step in range(1, row_size)]
    col_peers = [lax.rem(my_col + step, col_size) for step in range(1, col_size)]

    def row_copy(chunk, peer, source):
        part = pl.ds(chunk * size, size)
        return pltpu.make_async_remote_copy(
            src_ref=spectra.at[peer, part],
            dst_ref=row_recv.at[source, part],
            send_sem=row_send_sem.at[chunk, peer],
            recv_sem=row_recv_sem.at[chunk, source],
            device_id={"row": peer},
            device_id_type=MESH,
        )

    def row_own(chunk):
        part = pl.ds(chunk * size, size)
        return pltpu.make_async_copy(
            spectra.at[my_row, part], row_recv.at[my_row, part], row_own_sem.at[chunk]
        )

    def col_copy(chunk, peer, source):
        slot = lax.rem(chunk, SLOTS)
        return pltpu.make_async_remote_copy(
            src_ref=col_send.at[slot, peer],
            dst_ref=col_recv.at[source, pl.ds(chunk * size, size)],
            send_sem=col_send_sem.at[chunk, peer],
            recv_sem=col_recv_sem.at[chunk, source],
            device_id={"col": peer},
            device_id_type=MESH,
        )

    def col_own(chunk):
        return pltpu.make_async_copy(
            col_send.at[lax.rem(chunk, SLOTS), my_col],
            col_recv.at[my_col, pl.ds(chunk * size, size)],
            col_own_sem.at[chunk],
        )

    def start_row(chunk):
        for peer in row_peers:
            row_copy(chunk, peer, my_row).start()
        row_own(chunk).start()

    def combine(chunk):
        for peer in col_peers:
            col_copy(chunk, peer, peer).wait_recv()
        col_own(chunk).wait()

        def unit_step(step, carry):
            unit = chunk * size + step
            pol = unit // per_pol
            block = col_recv[:, unit].reshape(-1, width)
            real = jnp.dot(col_tab[:out_rows], block, preferred_element_type=F32)
            imag = jnp.dot(col_tab[out_rows:], block, preferred_element_type=F32)
            power[pol] += real * real + imag * imag
            return carry

        lax.fori_loop(0, size, unit_step, 0)

    barrier = pltpu.get_barrier_semaphore()
    for peer in row_peers:
        pl.semaphore_signal(barrier, inc=1, device_id={"row": peer}, device_id_type=MESH)
    for peer in col_peers:
        pl.semaphore_signal(barrier, inc=1, device_id={"col": peer}, device_id_type=MESH)
    pl.semaphore_wait(barrier, row_size + col_size - 2)

    power[...] = jnp.zeros_like(power)
    start_row(0)
    start_row(1)

    def chunk_step(chunk, carry):
        for peer in row_peers:
            row_copy(chunk, peer, peer).wait_recv()
        row_own(chunk).wait()

        @pl.when(chunk + 2 < chunks)
        def _():
            start_row(chunk + 2)

        @pl.when(chunk >= SLOTS)
        def _():
            for peer in col_peers:
                col_copy(chunk - SLOTS, peer, my_col).wait_send()

        slot = lax.rem(chunk, SLOTS)

        def unit_step(step, inner):
            for column in range(local_cols):
                block = row_recv[:, chunk * size + step, column].reshape(-1, width)
                beam = jnp.dot(row_tab[...], block, preferred_element_type=F32).astype(BF16)
                col_send[slot, :, step, column] = beam.reshape(col_size, -1, width)
            return inner

        lax.fori_loop(0, size, unit_step, 0)
        for peer in col_peers:
            col_copy(chunk, peer, my_col).start()
        col_own(chunk).start()

        @pl.when(chunk >= 1)
        def _():
            combine(chunk - 1)

        return carry

    lax.fori_loop(0, chunks, chunk_step, 0)
    combine(chunks - 1)

    def drain_row(chunk, carry):
        for peer in row_peers:
            row_copy(chunk, peer, my_row).wait_send()
        return carry

    def drain_col(chunk, carry):
        for peer in col_peers:
            col_copy(chunk, peer, my_col).wait_send()
        return carry

    lax.fori_loop(0, chunks, drain_row, 0)
    lax.fori_loop(chunks - SLOTS, chunks, drain_col, 0)


def form_beams(spectra, row_tab, col_tab, pols, row_size, col_size):
    _, units, local_cols, in_rows, width = spectra.shape
    nrow = row_tab.shape[0] // 2
    ncol = local_cols * col_size
    local_beams = nrow // col_size
    chunks = CHUNKS
    while units // pols % chunks and chunks > SLOTS + 1:
        chunks //= 2
    size = units // chunks
    vmem = pl.BlockSpec(memory_space=pltpu.VMEM)
    return pl.pallas_call(
        functools.partial(beam_kernel, row_size, col_size, chunks),
        in_specs=[pl.BlockSpec(memory_space=pl.ANY), vmem, vmem],
        out_specs=vmem,
        out_shape=jax.ShapeDtypeStruct((pols, local_beams * ncol, width), F32),
        scratch_shapes=[
            pltpu.VMEM((row_size, units, local_cols, in_rows, width), BF16),
            pltpu.VMEM((SLOTS, col_size, size, local_cols, 2 * local_beams, width), BF16),
            pltpu.VMEM((col_size, units, local_cols, 2 * local_beams, width), BF16),
            pltpu.SemaphoreType.DMA((chunks, row_size)),
            pltpu.SemaphoreType.DMA((chunks, row_size)),
            pltpu.SemaphoreType.DMA((chunks,)),
            pltpu.SemaphoreType.DMA((chunks, col_size)),
            pltpu.SemaphoreType.DMA((chunks, col_size)),
            pltpu.SemaphoreType.DMA((chunks,)),
        ],
        compiler_params=pltpu.CompilerParams(
            collective_id=0, has_side_effects=True, vmem_limit_bytes=VMEM_BYTES
        ),
        name="form_beams",
    )(spectra, row_tab, col_tab)


def body(voltages, fir):
    taps, nchan = fir.shape
    comps, local_rows, local_cols, pols, samples = voltages.shape
    row_size = lax.axis_size("row")
    col_size = lax.axis_size("col")
    nrow, ncol = local_rows * row_size, local_cols * col_size
    blocks = samples // nchan
    frames = blocks - taps + 1
    local_beams = nrow // col_size
    width = nchan // row_size
    volts = voltages.reshape(comps, local_rows, local_cols, pols, blocks, nchan)
    volts = volts.transpose(3, 2, 0, 4, 1, 5)
    spectra = channelize(volts, fir, jnp.asarray(channel_table(nchan, row_size)), row_size)
    spectra = spectra.reshape(row_size, pols * frames, local_cols, 2 * local_rows, width)
    power = form_beams(
        spectra,
        jnp.asarray(row_table(nrow, row_size, col_size)),
        jnp.asarray(col_table(ncol, col_size, local_beams)),
        pols, row_size, col_size,
    )
    scale = 1.0 / (frames * nrow * ncol)
    power = power.reshape(pols, local_beams, ncol, width) * scale
    return power.transpose(1, 2, 0, 3)


def solution(mesh):
    in_specs = (P(None, "row", "col", None, None), P())
    out_specs = P("col", None, None, "row")
    return jax.shard_map(body, mesh=mesh, in_specs=in_specs, out_specs=out_specs, check_vma=False)
```

time: 1360 us -> 589 us (0.43)
  Pallas kernels: 0 us -> 487 us
  blocking collectives: 368 us -> 0 us
  local copies, waits for them, and re-layouts: 396 us -> 98.8 us
  matrix products: 259 us -> 0 us
  waiting for transfers between devices: 181 us -> 0 us
  other arithmetic: 140 us -> 1.3 us
    pallas_call x0 -> x2, Pallas kernels: none -> 487 us  [the longest x1 401 us: form_beams(): pl.pallas_call(functools.partial(beam_kernel, row_size, col_size, chunks)...]
    all_to_all x1 -> x0, blocking collectives: 368 us -> none  [body(): lax.all_to_all(rowbeam, 'col', split_axis=1, concat_axis=2, tiled=True)]
    dot_general x3 -> x0, matrix products: 259 us -> none  [the longest x1 232 us: body(): jnp.einsum('cxn,cdnk->dxk', filtered, float_table(nchan), precision=lax.P...]
    slice x2 -> x0, local copies, waits for them, and re-layouts: 209 us -> none  [the longest x1 209 us: body(): shaped[:, :, :, :, tap:tap + frames, :].astype(jnp.float32) * fir[tap]]
    all_to_all x1 -> x0, waiting for transfers between devices: 181 us -> none  [body(): lax.all_to_all(spectra, 'row', split_axis=5, concat_axis=1, tiled=True)]
    add x1 -> x0, other arithmetic: 99.3 us -> none  [body(): filtered + shaped[:, :, :, :, tap:tap + frames, :].astype(jnp.float32) *...]
    convert_element_type x2 -> x0, local copies, waits for them, and re-layouts: 31.5 us -> none  [the longest x1 21.2 us: body(): channels.astype(jnp.bfloat16)]
    add x1 -> x0, local copies, waits for them, and re-layouts: 25.7 us -> none  [body(): filtered + shaped[:, :, :, :, tap:tap + frames, :].astype(jnp.float32) *...]
  transfers between devices with their start and end apart: 1 -> 0, of which waited for: 1 -> 0; matrix products, arithmetic and copies ran while one was open for 0% -> 0% of each run, Pallas kernels for 0% -> 0%
where the time goes in v1:
time: 589 us; the launch traced here: 587 us
  Pallas kernels  487 us (83%)
  local copies, waits for them, and re-layouts  98.8 us (17%)
    pallas_call x1, Pallas kernels, form_beams(): pl.pallas_call(functools.partial(beam_kernel, row_size, col_size, chunks)...  401 us
    reshape x2, local copies, waits for them, and re-layouts, body(): volts = voltages.reshape(comps, local_rows, local_cols, pols, blocks, nchan)  97 us
    pallas_call x1, Pallas kernels, channelize(): pl.pallas_call(channelize_kernel, grid=(pols, local_cols), in_specs=[pl.B...  85.7 us

profile of v1, /device:TPU:11, one launch (start us, length us, event | category | flops | bytes accessed | tf_op | source)
XLA Modules:
  0.0 587.3 jit_solution(5567763263983053076)
XLA Ops:
  0.0 66.1 %reshape.11 = bf16[2,16,8,2,31,1024]{5,4,3,2,1,0:T(8,128)(2,1)} reshape(bf16[2,16,8,2,31744]{4,3,2,1,0:T(2,128)(2,1)} %param.5) | data formatting | bytes 65011712 | tf_op jit(solution)/shard_map/reshape | solution.py:294
  66.1 30.9 %copy.14 = bf16[2,16,8,2,31,1024]{5,1,4,0,2,3:T(8,128)(2,1)} copy(bf16[2,16,8,2,31,1024]{5,4,3,2,1,0:T(8,128)(2,1)} %reshape.11) | data formatting | bytes 65011712 | tf_op jit(solution)/shard_map/reshape | solution.py:294
  97.0 85.7 %channelize.1 = bf16[4,2,16,8,32,256]{5,4,3,2,1,0:T(8,128)(2,1)} custom-call(bf16[2,8,2,31,16,1024]{5,4,3,2,1,0:T(8,128)(2,1)} %bitcast.8, f32[16,1024]{1,0:T(8,128)} %fir.1, bf16[2048,2048]{1,0:T(8,128)(2,1)} %constant.8.clone.table), custom_call_target="tpu_custom_call" | custom-call | tf_op jit(solution)/shard_map/channelize/pallas_call | solution.py:97
  182.7 401.5 %form_beams.1 = f32[2,512,256]{2,1,0:T(8,128)} custom-call(bf16[4,32,8,32,256]{4,3,2,1,0:T(8,128)(2,1)} %bitcast.9, bf16[128,128]{1,0:T(8,128)(2,1)} %constant.9.clone.row_tab, bf16[1024,1024]{1,0:T(8,128)(2,1)} %constant.10.clone.col_tab), custom_call_target="tpu_custom_call" | custom-call | tf_op jit(solution)/shard_map/form_beams/pallas_call | solution.py:261
  584.2 1.3 broadcast_multiply_fusion
  585.5 1.8 copy.15

commit v2 on v1

v2 whole, which is shorter than its diff:
```python
import functools
import math

import jax
import jax.numpy as jnp
import numpy as np
import ml_dtypes
from jax import lax
from jax.experimental import pallas as pl
from jax.experimental.pallas import tpu as pltpu
from jax.sharding import PartitionSpec as P

BF16 = jnp.bfloat16
F32 = jnp.float32
MESH = pl.DeviceIdType.MESH
VMEM_BYTES = 62 * 1024 * 1024
SLOTS = 3


def fourier_parts(length):
    index = np.arange(length)
    angle = (index[:, None] * index[None, :] % length).astype(np.float32) * np.float32(
        2.0 * math.pi / length
    )
    return np.cos(angle), np.sin(angle)


def channel_table(nchan):
    cosine, sine = fourier_parts(nchan)
    return np.concatenate([cosine, sine]).astype(ml_dtypes.bfloat16)


def spatial_parts(length):
    cosine, sine = fourier_parts(length)
    table = np.stack([np.stack([cosine, -sine]), np.stack([sine, cosine])])
    return table.astype(ml_dtypes.bfloat16)


def row_table(nrow, row_size, col_size):
    table = spatial_parts(nrow).reshape(2, 2, col_size, nrow // col_size, row_size, nrow // row_size)
    return table.transpose(2, 1, 3, 4, 0, 5).reshape(2 * nrow, 2 * nrow)


def col_table(ncol, col_size, local_beams):
    table = spatial_parts(ncol).astype(np.float32)
    eye = np.eye(local_beams, dtype=np.float32)
    full = np.einsum("cdvb,uw->duvbcw", table, eye)
    return full.reshape(2 * local_beams * ncol, ncol * 2 * local_beams).astype(ml_dtypes.bfloat16)


def beam_kernel(
    row_size, col_size, volts, fir, table, row_tab, col_tab, power,
    raw, spread, held, row_send, row_recv, col_send, col_recv,
    raw_sem, row_send_sem, row_recv_sem, row_own_sem, col_send_sem, col_recv_sem, col_own_sem,
):
    my_row = lax.axis_index("row")
    my_col = lax.axis_index("col")
    _, rows, local_cols, pols, _ = volts.shape
    taps, nchan = fir.shape
    blocks = spread.shape[0]
    frames = blocks - taps + 1
    lanes = spread.shape[3]
    tiles = nchan // lanes
    width = nchan // row_size
    out_rows = power.shape[1]
    chunks = pols * local_cols
    row_peers = [lax.rem(my_row + step, row_size) for step in range(1, row_size)]
    col_peers = [lax.rem(my_col + step, col_size) for step in range(1, col_size)]

    def raw_copy(chunk, comp):
        return pltpu.make_async_copy(
            volts.at[comp, :, lax.rem(chunk, local_cols)], raw.at[comp], raw_sem.at[comp]
        )

    def row_copy(chunk, peer, source):
        return pltpu.make_async_remote_copy(
            src_ref=row_send.at[lax.rem(chunk, SLOTS), peer],
            dst_ref=row_recv.at[source, chunk],
            send_sem=row_send_sem.at[chunk, peer],
            recv_sem=row_recv_sem.at[chunk, source],
            device_id={"row": peer},
            device_id_type=MESH,
        )

    def row_own(chunk):
        return pltpu.make_async_copy(
            row_send.at[lax.rem(chunk, SLOTS), my_row],
            row_recv.at[my_row, chunk],
            row_own_sem.at[chunk],
        )

    def col_copy(chunk, peer, source):
        return pltpu.make_async_remote_copy(
            src_ref=col_send.at[lax.rem(chunk, SLOTS), peer],
            dst_ref=col_recv.at[source, chunk],
            send_sem=col_send_sem.at[chunk, peer],
            recv_sem=col_recv_sem.at[chunk, source],
            device_id={"col": peer},
            device_id_type=MESH,
        )

    def col_own(chunk):
        return pltpu.make_async_copy(
            col_send.at[lax.rem(chunk, SLOTS), my_col],
            col_recv.at[my_col, chunk],
            col_own_sem.at[chunk],
        )

    def channelize(chunk):
        pol = chunk // local_cols
        for comp in range(2):
            raw_copy(chunk, comp).wait()

            def spread_step(block, carry):
                start = pl.multiple_of(block * nchan, nchan)
                for row in range(rows):
                    pair = raw[comp, row, :, pl.ds(start, nchan)].astype(F32)
                    for tile in range(tiles):
                        spread[block, tile, pl.ds(row, pols, stride=rows), :] = pair[
                            :, tile * lanes : (tile + 1) * lanes
                        ]
                return carry

            lax.fori_loop(0, blocks, spread_step, 0)

            @pl.when(chunk + 1 < chunks)
            def _():
                raw_copy(chunk + 1, comp).start()

            def filter_step(tile, carry):
                start = pl.multiple_of(tile * lanes, lanes)
                weights = [
                    jnp.broadcast_to(fir[pl.ds(tap, 1), pl.ds(start, lanes)], (rows, lanes))
                    for tap in range(taps)
                ]
                first = pl.multiple_of(pol * rows, rows)
                values = [spread[block, tile, pl.ds(first, rows), :] for block in range(blocks)]
                for frame in range(frames):
                    total = values[frame] * weights[0]
                    for tap in range(1, taps):
                        total = total + values[frame + tap] * weights[tap]
                    held[frame, :, pl.ds(pl.multiple_of(comp * nchan + start, lanes), lanes)] = (
                        total.astype(BF16)
                    )
                    if comp == 0:
                        held[frame, :, pl.ds(pl.multiple_of(2 * nchan + start, lanes), lanes)] = (
                            -total
                        ).astype(BF16)
                return carry

            lax.fori_loop(0, tiles, filter_step, 0)

        @pl.when(chunk >= SLOTS)
        def _():
            for peer in row_peers:
                row_copy(chunk - SLOTS, peer, my_row).wait_send()

        slot = lax.rem(chunk, SLOTS)
        for comp in range(2):
            lead = held[:, :, comp * nchan : (comp + 2) * nchan].reshape(frames * rows, 2 * nchan)
            for dest in range(row_size):
                part = jnp.dot(
                    lead, table[:, dest * width : (dest + 1) * width], preferred_element_type=F32
                ).astype(BF16)
                row_send[slot, dest, :, comp * rows : (comp + 1) * rows, :] = part.reshape(
                    frames, rows, width
                )

        for peer in row_peers:
            row_copy(chunk, peer, my_row).start()
        row_own(chunk).start()

    def form_rows(chunk):
        for peer in row_peers:
            row_copy(chunk, peer, peer).wait_recv()
        row_own(chunk).wait()

        @pl.when(chunk >= SLOTS)
        def _():
            for peer in col_peers:
                col_copy(chunk - SLOTS, peer, my_col).wait_send()
            col_own(chunk - SLOTS).wait()

        slot = lax.rem(chunk, SLOTS)

        def frame_step(step, carry):
            for part in range(4):
                frame = step * 4 + part
                block = row_recv[:, chunk, frame].reshape(-1, width)
                beam = jnp.dot(row_tab[...], block, preferred_element_type=F32).astype(BF16)
                col_send[slot, :, frame] = beam.reshape(col_size, -1, width)
            return carry

        lax.fori_loop(0, frames // 4, frame_step, 0)
        for peer in col_peers:
            col_copy(chunk, peer, my_col).start()
        col_own(chunk).start()

    def combine(pol):
        def receive(chunk, carry):
            for peer in col_peers:
                col_copy(chunk, peer, peer).wait_recv()
            return carry

        lax.fori_loop(pol * local_cols, (pol + 1) * local_cols, receive, 0)

        def frame_step(frame, carry):
            block = col_recv[:, pol * local_cols : (pol + 1) * local_cols, frame].reshape(-1, width)
            real = jnp.dot(col_tab[:out_rows], block, preferred_element_type=F32)
            imag = jnp.dot(col_tab[out_rows:], block, preferred_element_type=F32)
            power[pol] += real * real + imag * imag
            return carry

        lax.fori_loop(0, frames, frame_step, 0)

    for comp in range(2):
        raw_copy(0, comp).start()
    barrier = pltpu.get_barrier_semaphore()
    for peer in row_peers:
        pl.semaphore_signal(barrier, inc=1, device_id={"row": peer}, device_id_type=MESH)
    for peer in col_peers:
        pl.semaphore_signal(barrier, inc=1, device_id={"col": peer}, device_id_type=MESH)
    pl.semaphore_wait(barrier, row_size + col_size - 2)
    power[...] = jnp.zeros_like(power)

    def chunk_step(chunk, carry):
        @pl.when(chunk < chunks)
        def _():
            channelize(chunk)

        @pl.when(chunk >= 1)
        def _():
            form_rows(chunk - 1)

        for pol in range(pols - 1):
            @pl.when(chunk == (pol + 1) * local_cols + SLOTS)
            def _():
                combine(pol)

        return carry

    lax.fori_loop(0, chunks + 1, chunk_step, 0)

    def drain(chunk, carry):
        for peer in row_peers:
            row_copy(chunk, peer, my_row).wait_send()
        for peer in col_peers:
            col_copy(chunk, peer, my_col).wait_send()
        col_own(chunk).wait()
        return carry

    lax.fori_loop(chunks - SLOTS, chunks, drain, 0)
    combine(pols - 1)


def form_beams(voltages, fir, table, row_tab, col_tab, row_size, col_size):
    _, rows, local_cols, pols, samples = voltages.shape
    taps, nchan = fir.shape
    blocks = samples // nchan
    frames = blocks - taps + 1
    width = nchan // row_size
    lanes = 128
    ncol = local_cols * col_size
    local_beams = rows * row_size // col_size
    chunks = pols * local_cols
    vmem = pl.BlockSpec(memory_space=pltpu.VMEM)
    return pl.pallas_call(
        functools.partial(beam_kernel, row_size, col_size),
        in_specs=[pl.BlockSpec(memory_space=pl.ANY), vmem, vmem, vmem, vmem],
        out_specs=vmem,
        out_shape=jax.ShapeDtypeStruct((pols, local_beams * ncol, width), F32),
        scratch_shapes=[
            pltpu.VMEM((2, rows, pols, samples), BF16),
            pltpu.VMEM((blocks, nchan // lanes, pols * rows, lanes), F32),
            pltpu.VMEM((frames, rows, 3 * nchan), BF16),
            pltpu.VMEM((SLOTS, row_size, frames, 2 * rows, width), BF16),
            pltpu.VMEM((row_size, chunks, frames, 2 * rows, width), BF16),
            pltpu.VMEM((SLOTS, col_size, frames, 2 * local_beams, width), BF16),
            pltpu.VMEM((col_size, chunks, frames, 2 * local_beams, width), BF16),
            pltpu.SemaphoreType.DMA((2,)),
            pltpu.SemaphoreType.DMA((chunks, row_size)),
            pltpu.SemaphoreType.DMA((chunks, row_size)),
            pltpu.SemaphoreType.DMA((chunks,)),
            pltpu.SemaphoreType.DMA((chunks, col_size)),
            pltpu.SemaphoreType.DMA((chunks, col_size)),
            pltpu.SemaphoreType.DMA((chunks,)),
        ],
        compiler_params=pltpu.CompilerParams(
            collective_id=0, has_side_effects=True, vmem_limit_bytes=VMEM_BYTES
        ),
        name="form_beams",
    )(voltages, fir, table, row_tab, col_tab)


def body(voltages, fir):
    taps, nchan = fir.shape
    _, local_rows, local_cols, pols, samples = voltages.shape
    row_size = lax.axis_size("row")
    col_size = lax.axis_size("col")
    nrow, ncol = local_rows * row_size, local_cols * col_size
    frames = samples // nchan - taps + 1
    local_beams = nrow // col_size
    power = form_beams(
        voltages, fir,
        jnp.asarray(channel_table(nchan)),
        jnp.asarray(row_table(nrow, row_size, col_size)),
        jnp.asarray(col_table(ncol, col_size, local_beams)),
        row_size, col_size,
    )
    scale = 1.0 / (frames * nrow * ncol)
    power = power.reshape(pols, local_beams, ncol, nchan // row_size) * scale
    return power.transpose(1, 2, 0, 3)


def solution(mesh):
    in_specs = (P(None, "row", "col", None, None), P())
    out_specs = P("col", None, None, "row")
    return jax.shard_map(body, mesh=mesh, in_specs=in_specs, out_specs=out_specs, check_vma=False)
```

time: 589 us -> 409 us (0.69)
  local copies, waits for them, and re-layouts: 98.8 us -> 1.78 us
  Pallas kernels: 487 us -> 405 us
    reshape x2 -> x0, local copies, waits for them, and re-layouts: 97 us -> none  [body(): volts = voltages.reshape(comps, local_rows, local_cols, pols, blocks, nchan)]
    pallas_call x2 -> x1, Pallas kernels: 487 us -> 405 us  [form_beams(): pl.pallas_call(functools.partial(beam_kernel, row_size, col_size), in_spe...]
where the time goes in v2:
time: 409 us; the launch traced here: 408 us
  Pallas kernels  405 us (99%)
    pallas_call x1, Pallas kernels, form_beams(): pl.pallas_call(functools.partial(beam_kernel, row_size, col_size), in_spe...  405 us

profile of v2, /device:TPU:11, one launch (start us, length us, event | category | flops | bytes accessed | tf_op | source)
XLA Modules:
  0.0 408.4 jit_solution(14823100438449069610)
XLA Ops:
  0.0 405.3 %form_beams.1 = f32[2,512,256]{2,1,0:T(8,128)} custom-call(bf16[2,16,8,2,31744]{4,3,2,1,0:T(2,128)(2,1)} %volts.1, f32[16,1024]{1,0:T(8,128)} %fir.1, bf16[2048,1024]{1,0:T(8,128)(2,1)} %constant.8.clone.table, bf16[128,128]{1,0:T(8,128)(2,1)} %constant.9.clone.row_tab, bf16[1024,1024]{1,0:T(8,128)(2,1)} %constant.10.clone.col_tab), custom_call_target="tpu_custom_call" | custom-call | tf_op jit(solution)/shard_map/form_beams/pallas_call | solution.py:267
  405.3 1.3 broadcast_multiply_fusion
  406.6 1.8 copy.8
